TPU v7x, 32 devices: a whole 2x2x4 slice. The times are simulated.
32 devices in a mesh: sub: 4 (over y, core), blk: 8 (over z, x).
Axes of the slice: x: 2, y: 2, z: 4, core: 2. Of those that a mesh axis runs over, the one named last changes fastest.
Arguments:
- face_loads: float32 [32, 5, 256, 128], P(('sub', 'blk')), may hold values from -6 to 6
- edge_mask: int32 [32, 5], P(('sub', 'blk')), may hold values from 0 to 1, as said below
- dof_map: int32 [32, 5, 256], P(('sub', 'blk')), may hold values from 0 to 255, as said below
- dual_op: float32 [32, 1280, 1280], P(('sub', 'blk')), as said below
- dirichlet: float32 [32, 1280, 1280], P(('sub', 'blk')), as said below
- coupling: float32 [32, 48, 1280], P(('sub', 'blk')), may hold values from -0.3125 to 0.3125
- corner_map: int32 [32, 48], replicated, may hold values from 0 to 1535, all different within a row
- coarse_inv: float32 [1536, 1536], P('blk'), as said below
Outputs:
- multipliers: float32 [32, 5, 256, 128], P(('sub', 'blk'))
- residual: float32 [32, 5, 256, 128], P(('sub', 'blk'))
Inputs may be any that keep to these rules, and one draw needn't show every extreme that they name: edge_mask[s, r] equals edge_mask[partner(s, r), r]. Each dof_map[s, r] is a permutation of the 256 face unknowns, and dof_map[partner(s, r), r] is its inverse. Each dual_op[s] is symmetric positive definite. Each dirichlet[s] is symmetric positive definite. `coarse_inv`: symmetric positive definite. `corner_map`: a subdomain names 48 different coarse unknowns.
All inputs are finite; a program needn't handle non-finite values.
Results may differ from a plain program's by a relative error of at most 0.0003.
Values sent between devices are 32-bit elements; how exact they have to be, the bound alone decides.
A program may use at most 128 MiB of HBM per device.

v0:
```python
import jax
import jax.numpy as jnp
from jax import lax
from jax.sharding import PartitionSpec as P

ITERS = 2


def from_partner(array, axis, distance):
    return lax.ppermute(array, axis, [(i, i ^ 1 << distance) for i in range(lax.axis_size(axis))])


def local_apply(matrix, vector):
    shaped = vector.reshape(matrix.shape[1], vector.shape[-1])
    result = jnp.dot(
        matrix, shaped, precision=lax.Precision.HIGHEST, preferred_element_type=jnp.float32
    )
    return result.reshape(vector.shape)


def shards(face_loads, edge_mask, dof_map, dual_op, dirichlet, coupling, corner_map, coarse_inv):
    highest = lax.Precision.HIGHEST
    contract_first = (((0,), (0,)), ((), ()))
    mask_row = edge_mask[0].astype(jnp.float32)
    perm_rows = dof_map[0]
    colours = face_loads.shape[1]
    blk_count = lax.axis_size("blk")
    own_index = lax.axis_index("sub") * blk_count + lax.axis_index("blk")
    own_map = lax.dynamic_slice_in_dim(corner_map, own_index, 1, 0)[0]
    coarse_total = coarse_inv.shape[1]
    coupler = coupling[0]

    def assemble(vector):
        pieces = []
        for colour in range(colours):
            face_part = vector[colour]
            if colour < 3:
                facing = from_partner(face_part, "blk", colour)
            else:
                facing = from_partner(face_part, "sub", colour - 3)
            remote = jnp.take(facing, perm_rows[colour], axis=0)
            pieces.append(mask_row[colour] * (face_part - remote))
        return jnp.stack(pieces)

    def precondition(vector):
        return assemble(local_apply(dirichlet[0], vector))

    def reduce_rz(left, right):
        return lax.psum(jnp.sum(left * right, axis=(0, 1)), ("sub", "blk"))

    residual = assemble(face_loads[0])
    multipliers = jnp.zeros_like(residual)
    precond = precondition(residual)
    direction = precond
    inner_rz = reduce_rz(residual, precond)
    for sweep_idx in range(ITERS):
        shaped = direction.reshape(coupler.shape[1], direction.shape[-1])
        partial_corner = jnp.dot(
            coupler, shaped, precision=highest, preferred_element_type=jnp.float32
        )
        columns = jnp.arange(coarse_total, dtype=jnp.int32)
        selector = (own_map[:, None] == columns[None, :]).astype(jnp.float32)
        spread = lax.dot_general(selector, partial_corner, contract_first, precision=highest)
        summed = lax.psum(spread, ("sub", "blk"))
        solved = jnp.dot(coarse_inv, summed, precision=highest, preferred_element_type=jnp.float32)
        whole = lax.all_gather(solved, "blk", axis=0, tiled=True)
        corner_values = jnp.take(whole, own_map, axis=0)
        back = lax.dot_general(coupler, corner_values, contract_first, precision=highest)
        image = assemble(local_apply(dual_op[0], direction) + back.reshape(direction.shape))
        curvature = lax.psum(jnp.sum(direction * image, axis=(0, 1)), ("sub", "blk"))
        alpha = inner_rz / curvature
        multipliers = multipliers + alpha * direction
        residual = residual - alpha * image
        if sweep_idx + 1 < ITERS:
            precond = precondition(residual)
            rz_next = reduce_rz(residual, precond)
            direction = precond + rz_next / inner_rz * direction
            inner_rz = rz_next
    return (multipliers[None], residual[None])


def solution(mesh):
    placed = (
        P(("sub", "blk"), None, None, None),
        P(("sub", "blk"), None),
        P(("sub", "blk"), None, None),
        P(("sub", "blk"), None, None),
        P(("sub", "blk"), None, None),
        P(("sub", "blk"), None, None),
        P(),
        P("blk", None),
    )
    return jax.shard_map(
        shards,
        mesh=mesh,
        in_specs=placed,
        out_specs=(P(("sub", "blk"), None, None, None), P(("sub", "blk"), None, None, None)),
        check_vma=False,
    )
```

profile of v0, /device:TPU:0, one launch (start us, length us, event | category | flops | bytes accessed | tf_op | source)
XLA Modules:
  0.0 686.9 jit_solution(11943507902904656700)
XLA Ops:
  8.6 3.0 collective-permute-start
  13.5 2.7 collective-permute-start.2
  28.5 8.4 %fusion.20 = f32[1280,128]{0,1:T(8,128)S(1)} fusion(f32[1280,128]{1,0:T(8,128)S(1)} %bitcast.191, f32[1,1280,1280]{2,1,0:T(8,128)} %param.16), kind=kOutput, calls=%fused_computation.39 | convolution fusion | flops 2516582400 | bytes 7864320 | tf_op jit(solution)/shard_map/dot_general | solution.py:15
  39.1 2.9 collective-permute-start.6
  63.8 2.3 fusion.33
  69.7 125.1 %all-reduce.4.cloned.1.call-done = f32[1536,128]{1,0:T(8,128)} async-done(((f32[1536,128]{1,0:T(8,128)}), f32[1536,128]{1,0:T(8,128)}) %all-reduce.4.cloned.1.call-update) | async-done | bytes 786448 | tf_op jit(solution)/shard_map/psum | solution.py:64
  194.8 2.2 convolution_bitcast_fusion.1
  197.0 34.0 %all_gather.6 = f32[1536,128]{1,0:T(8,128)} all-gather(f32[192,128]{1,0:T(8,128)S(1)} %convolution_bitcast_fusion.1), channel_id=1, replica_groups=mesh['sub'=4,'blk'=8] {'blk'}, dimensions={0}, use_global_device_ids=true | all-gather | bytes 884736 | tf_op jit(solution)/shard_map/all_gather | solution.py:66
  234.2 8.6 %fusion.17 = f32[1280,128]{0,1:T(8,128)S(1)} fusion(f32[128,1280]{1,0:T(8,128)S(1)} %fusion.31, f32[1280,128]{1,0:T(8,128)} %bitcast.188, f32[1,1280,1280]{2,1,0:T(8,128)} %param.15), kind=kOutput, calls=%fused_computation.38 | convolution fusion | flops 2516746240 | bytes 8519680 | tf_op jit(solution)/shard_map/dot_general | solution.py:15
  246.3 2.3 collective-permute-start.10
  278.0 38.2 %all-reduce = (f32[128]{0:T(128)}, f32[128]{0:T(128)}) all-reduce(f32[128]{0:T(128)} %get-tuple-element.9, f32[128]{0:T(128)} %get-tuple-element.8), channel_id=1, replica_groups=mesh['sub'=4,'blk'=8] {'sub','blk'}, use_global_device_ids=true, to_apply=%region_1.3 | all-reduce | flops 256 | bytes 2048 | tf_op jit(solution)/shard_map/psum | solution.py:49
  319.5 2.2 copy.104
  321.7 8.6 %fusion.23 = f32[1280,128]{0,1:T(8,128)S(1)} fusion(f32[1280,128]{1,0:T(8,128)} %bitcast.192, f32[1,1280,1280]{2,1,0:T(8,128)} %param.16), kind=kOutput, calls=%fused_computation.40 | convolution fusion | flops 2516582400 | bytes 7864320 | tf_op jit(solution)/shard_map/dot_general | solution.py:15
  331.2 2.5 collective-permute-start.19
  333.7 2.9 collective-permute-start.17
  366.9 40.0 %psum.45 = f32[128]{0:T(128)S(1)} all-reduce(f32[128]{0:T(128)S(1)} %multiply_reduce_fusion.1), channel_id=1, replica_groups=mesh['sub'=4,'blk'=8] {'sub','blk'}, use_global_device_ids=true, to_apply=%region_6.9 | all-reduce | flops 128 | bytes 1024 | tf_op jit(solution)/shard_map/psum | solution.py:49
  407.6 2.3 multiply_add_fusion.1
  413.9 129.0 %all-reduce.6.cloned.1.call-done = f32[1536,128]{1,0:T(8,128)} async-done(((f32[1536,128]{1,0:T(8,128)}), f32[1536,128]{1,0:T(8,128)}) %all-reduce.6.cloned.1.call-update) | async-done | bytes 786448 | tf_op jit(solution)/shard_map/psum | solution.py:64
  542.9 2.2 convolution_bitcast_fusion
  545.1 34.2 %all_gather.7 = f32[1536,128]{1,0:T(8,128)} all-gather(f32[192,128]{1,0:T(8,128)S(1)} %convolution_bitcast_fusion), channel_id=1, replica_groups=mesh['sub'=4,'blk'=8] {'blk'}, dimensions={0}, use_global_device_ids=true | all-gather | bytes 884736 | tf_op jit(solution)/shard_map/all_gather | solution.py:66
  582.6 8.6 %fusion.14 = f32[1280,128]{0,1:T(8,128)S(1)} fusion(f32[128,1280]{1,0:T(8,128)S(1)} %fusion.27, f32[1280,128]{1,0:T(8,128)} %bitcast.190, f32[1,1280,1280]{2,1,0:T(8,128)} %param.15), kind=kOutput, calls=%fused_computation.37 | convolution fusion | flops 2516746240 | bytes 8519680 | tf_op jit(solution)/shard_map/dot_general | solution.py:15
  593.7 3.3 collective-permute-start.21
  607.6 2.7 bitcast_dynamic-update-slice_fusion.9
  616.2 2.1 bitcast_dynamic-update-slice_fusion.23
  618.4 2.1 bitcast_dynamic-update-slice_fusion.22
  620.5 2.2 bitcast_dynamic-update-slice_fusion.21
  626.3 37.7 %psum.47 = f32[128]{0:T(128)} all-reduce(f32[128]{0:T(128)S(1)} %multiply_reduce_fusion), channel_id=1, replica_groups=mesh['sub'=4,'blk'=8] {'sub','blk'}, use_global_device_ids=true, to_apply=%region_9.12 | all-reduce | flops 128 | bytes 1024 | tf_op jit(solution)/shard_map/psum | solution.py:70
  664.7 2.7 bitcast_dynamic-update-slice_fusion.8
  667.3 2.7 bitcast_dynamic-update-slice_fusion.7
  670.0 2.7 bitcast_dynamic-update-slice_fusion.6
  672.7 2.6 bitcast_dynamic-update-slice_fusion.5
  675.2 2.3 multiply_subtract_fusion
  (270 shorter events, 146.3 us)
Async XLA Ops:
  7.2 187.6 %all-reduce.4.cloned.1.call-start = ((), (), s32[]{:S(2)}) async-start(), calls=%async_computation | async-start | bytes 1572864 | tf_op jit(solution)/shard_map/psum | solution.py:64
  8.6 11.7 %collective-permute-start = (f32[256,128]{0,1:T(8,128)S(1)}, f32[256,128]{0,1:T(8,128)S(1)}, u32[]{:S(2)}, u32[]{:S(2)}) collective-permute-start(f32[256,128]{0,1:T(8,128)S(1)} %bitcast.197), channel_id=1, source_target_pairs={{0,1},{1,0},{2,3},{3,2},{4,5},{5,4},{6,7},{7,6},{8,9},{9,8},{10,11... | collective-permute-start | bytes 393224 | tf_op jit(solution)/shard_map/ppermute | solution.py:10
  11.7 9.6 %collective-permute-start.1 = (f32[256,128]{0,1:T(8,128)S(1)}, f32[256,128]{0,1:T(8,128)S(1)}, u32[]{:S(2)}, u32[]{:S(2)}) collective-permute-start(f32[256,128]{0,1:T(8,128)S(1)} %bitcast.196), channel_id=1, source_target_pairs={{0,2},{1,3},{2,0},{3,1},{4,6},{5,7},{6,4},{7,5},{8,10},{9,11},{10,... | collective-permute-start | bytes 393224 | tf_op jit(solution)/shard_map/ppermute | solution.py:10
  13.5 8.8 %collective-permute-start.2 = (f32[256,128]{0,1:T(8,128)S(1)}, f32[256,128]{0,1:T(8,128)S(1)}, u32[]{:S(2)}, u32[]{:S(2)}) collective-permute-start(f32[256,128]{0,1:T(8,128)S(1)} %bitcast.195), channel_id=1, source_target_pairs={{0,4},{1,5},{2,6},{3,7},{4,0},{5,1},{6,2},{7,3},{8,12},{9,13},{10,... | collective-permute-start | bytes 393224 | tf_op jit(solution)/shard_map/ppermute | solution.py:10
  16.3 6.9 %collective-permute-start.3 = (f32[256,128]{0,1:T(8,128)S(1)}, f32[256,128]{0,1:T(8,128)S(1)}, u32[]{:S(2)}, u32[]{:S(2)}) collective-permute-start(f32[256,128]{0,1:T(8,128)S(1)} %bitcast.194), channel_id=1, source_target_pairs={{0,8},{8,0},{16,24},{24,16},{1,9},{9,1},{17,25},{25,17},{2,10},{10... | collective-permute-start | bytes 393224 | tf_op jit(solution)/shard_map/ppermute | solution.py:10
  16.5 7.7 %collective-permute-start.4 = (f32[256,128]{0,1:T(8,128)S(1)}, f32[256,128]{0,1:T(8,128)S(1)}, u32[]{:S(2)}, u32[]{:S(2)}) collective-permute-start(f32[256,128]{0,1:T(8,128)S(1)} %bitcast.193), channel_id=1, source_target_pairs={{0,16},{8,24},{16,0},{24,8},{1,17},{9,25},{17,1},{25,9},{2,18},{10... | collective-permute-start | bytes 393224 | tf_op jit(solution)/shard_map/ppermute | solution.py:10
  18.8 341.5 %copy-start.30 = (pred[256]{0:T(512)(128)(4,1)}, pred[256]{0:T(512)(128)(4,1)S(1)}, u32[]{:S(2)}) copy-start(pred[256]{0:T(512)(128)(4,1)S(1)} %compare_and_fusion.3) | copy-start | bytes 772
  18.8 344.5 %copy-start.26 = (pred[256]{0:T(512)(128)(4,1)}, pred[256]{0:T(512)(128)(4,1)S(1)}, u32[]{:S(2)}) copy-start(pred[256]{0:T(512)(128)(4,1)S(1)} %compare_and_fusion.1) | copy-start | bytes 772
  18.9 342.8 %copy-start.28 = (pred[256]{0:T(512)(128)(4,1)}, pred[256]{0:T(512)(128)(4,1)S(1)}, u32[]{:S(2)}) copy-start(pred[256]{0:T(512)(128)(4,1)S(1)} %compare_and_fusion.2) | copy-start | bytes 772
  19.0 324.1 %copy-start.24 = (s32[1024]{0:T(1024)}, s32[1024]{0:T(1024)S(1)}, u32[]{:S(2)}) copy-start(s32[1024]{0:T(1024)S(1)} %pad_clamp_fusion.2) | copy-start | bytes 12292
  19.0 328.1 %copy-start.23 = (s32[1024]{0:T(1024)}, s32[1024]{0:T(1024)S(1)}, u32[]{:S(2)}) copy-start(s32[1024]{0:T(1024)S(1)} %pad_clamp_fusion.3) | copy-start | bytes 12292
  37.6 6.0 collective-permute-start.9
  38.9 5.7 collective-permute-start.8
  38.9 9.7 %collective-permute-start.7 = (f32[256,128]{0,1:T(8,128)S(1)}, f32[256,128]{0,1:T(8,128)}, u32[]{:S(2)}, u32[]{:S(2)}) collective-permute-start(f32[256,128]{0,1:T(8,128)S(1)} %get-tuple-element.31), channel_id=1, source_target_pairs={{0,4},{1,5},{2,6},{3,7},{4,0},{5,1},{6,2},{7,3},{8,12},{9,13},{10,... | collective-permute-start | bytes 393224 | tf_op jit(solution)/shard_map/ppermute | solution.py:10
  39.1 12.0 %collective-permute-start.6 = (f32[256,128]{0,1:T(8,128)S(1)}, f32[256,128]{0,1:T(8,128)}, u32[]{:S(2)}, u32[]{:S(2)}) collective-permute-start(f32[256,128]{0,1:T(8,128)S(1)} %get-tuple-element.32), channel_id=1, source_target_pairs={{0,2},{1,3},{2,0},{3,1},{4,6},{5,7},{6,4},{7,5},{8,10},{9,11},{10,... | collective-permute-start | bytes 393224 | tf_op jit(solution)/shard_map/ppermute | solution.py:10
  41.9 11.6 %collective-permute-start.5 = (f32[256,128]{0,1:T(8,128)S(1)}, f32[256,128]{0,1:T(8,128)}, u32[]{:S(2)}, u32[]{:S(2)}) collective-permute-start(f32[256,128]{0,1:T(8,128)S(1)} %get-tuple-element.33), channel_id=1, source_target_pairs={{0,1},{1,0},{2,3},{3,2},{4,5},{5,4},{6,7},{7,6},{8,9},{9,8},{10,11... | collective-permute-start | bytes 393224 | tf_op jit(solution)/shard_map/ppermute | solution.py:10
  68.2 474.6 %all-reduce.6.cloned.1.call-start = ((), (), s32[]{:S(2)}) async-start(), calls=%async_computation.1 | async-start | bytes 1572864 | tf_op jit(solution)/shard_map/psum | solution.py:64
  243.6 5.1 collective-permute-start.14
  245.1 7.6 %collective-permute-start.13 = (f32[256,128]{0,1:T(8,128)}, f32[256,128]{0,1:T(8,128)}, u32[]{:S(2)}, u32[]{:S(2)}) collective-permute-start(f32[256,128]{0,1:T(8,128)} %get-tuple-element.25), channel_id=1, source_target_pairs={{0,8},{8,0},{16,24},{24,16},{1,9},{9,1},{17,25},{25,17},{2,10},{10... | collective-permute-start | bytes 393224 | tf_op jit(solution)/shard_map/ppermute | solution.py:10
  245.1 11.6 %collective-permute-start.12 = (f32[256,128]{0,1:T(8,128)}, f32[256,128]{0,1:T(8,128)}, u32[]{:S(2)}, u32[]{:S(2)}) collective-permute-start(f32[256,128]{0,1:T(8,128)} %get-tuple-element.26), channel_id=1, source_target_pairs={{0,4},{1,5},{2,6},{3,7},{4,0},{5,1},{6,2},{7,3},{8,12},{9,13},{10,... | collective-permute-start | bytes 393224 | tf_op jit(solution)/shard_map/ppermute | solution.py:10
  245.1 15.6 %collective-permute-start.11 = (f32[256,128]{0,1:T(8,128)}, f32[256,128]{0,1:T(8,128)}, u32[]{:S(2)}, u32[]{:S(2)}) collective-permute-start(f32[256,128]{0,1:T(8,128)} %get-tuple-element.27), channel_id=1, source_target_pairs={{0,2},{1,3},{2,0},{3,1},{4,6},{5,7},{6,4},{7,5},{8,10},{9,11},{10,... | collective-permute-start | bytes 393224 | tf_op jit(solution)/shard_map/ppermute | solution.py:10
  246.3 18.5 %collective-permute-start.10 = (f32[256,128]{0,1:T(8,128)}, f32[256,128]{0,1:T(8,128)}, u32[]{:S(2)}, u32[]{:S(2)}) collective-permute-start(f32[256,128]{0,1:T(8,128)} %get-tuple-element.28), channel_id=1, source_target_pairs={{0,1},{1,0},{2,3},{3,2},{4,5},{5,4},{6,7},{7,6},{8,9},{9,8},{10,11... | collective-permute-start | bytes 393224 | tf_op jit(solution)/shard_map/ppermute | solution.py:10
  331.2 6.9 %collective-permute-start.19 = (f32[256,128]{0,1:T(8,128)S(1)}, f32[256,128]{0,1:T(8,128)}, u32[]{:S(2)}, u32[]{:S(2)}) collective-permute-start(f32[256,128]{0,1:T(8,128)S(1)} %get-tuple-element.19), channel_id=1, source_target_pairs={{0,16},{8,24},{16,0},{24,8},{1,17},{9,25},{17,1},{25,9},{2,18},{10... | collective-permute-start | bytes 393224 | tf_op jit(solution)/shard_map/ppermute | solution.py:10
  333.7 8.4 %collective-permute-start.18 = (f32[256,128]{0,1:T(8,128)}, f32[256,128]{0,1:T(8,128)}, u32[]{:S(2)}, u32[]{:S(2)}) collective-permute-start(f32[256,128]{0,1:T(8,128)} %get-tuple-element.20), channel_id=1, source_target_pairs={{0,8},{8,0},{16,24},{24,16},{1,9},{9,1},{17,25},{25,17},{2,10},{10... | collective-permute-start | bytes 393224 | tf_op jit(solution)/shard_map/ppermute | solution.py:10
  333.7 12.4 %collective-permute-start.17 = (f32[256,128]{0,1:T(8,128)}, f32[256,128]{0,1:T(8,128)}, u32[]{:S(2)}, u32[]{:S(2)}) collective-permute-start(f32[256,128]{0,1:T(8,128)} %get-tuple-element.21), channel_id=1, source_target_pairs={{0,4},{1,5},{2,6},{3,7},{4,0},{5,1},{6,2},{7,3},{8,12},{9,13},{10,... | collective-permute-start | bytes 393224 | tf_op jit(solution)/shard_map/ppermute | solution.py:10
  336.7 13.5 %collective-permute-start.16 = (f32[256,128]{0,1:T(8,128)}, f32[256,128]{0,1:T(8,128)}, u32[]{:S(2)}, u32[]{:S(2)}) collective-permute-start(f32[256,128]{0,1:T(8,128)} %get-tuple-element.22), channel_id=1, source_target_pairs={{0,2},{1,3},{2,0},{3,1},{4,6},{5,7},{6,4},{7,5},{8,10},{9,11},{10,... | collective-permute-start | bytes 393224 | tf_op jit(solution)/shard_map/ppermute | solution.py:10
  336.7 17.5 %collective-permute-start.15 = (f32[256,128]{0,1:T(8,128)}, f32[256,128]{0,1:T(8,128)}, u32[]{:S(2)}, u32[]{:S(2)}) collective-permute-start(f32[256,128]{0,1:T(8,128)} %get-tuple-element.23), channel_id=1, source_target_pairs={{0,1},{1,0},{2,3},{3,2},{4,5},{5,4},{6,7},{7,6},{8,9},{9,8},{10,11... | collective-permute-start | bytes 393224 | tf_op jit(solution)/shard_map/ppermute | solution.py:10
  592.0 5.0 collective-permute-start.24
  593.5 5.2 collective-permute-start.23
  593.5 8.0 %collective-permute-start.22 = (f32[256,128]{0,1:T(8,128)S(1)}, f32[256,128]{0,1:T(8,128)}, u32[]{:S(2)}, u32[]{:S(2)}) collective-permute-start(f32[256,128]{0,1:T(8,128)S(1)} %get-tuple-element.16), channel_id=1, source_target_pairs={{0,4},{1,5},{2,6},{3,7},{4,0},{5,1},{6,2},{7,3},{8,12},{9,13},{10,... | collective-permute-start | bytes 393224 | tf_op jit(solution)/shard_map/ppermute | solution.py:10
  593.5 10.7 %collective-permute-start.20 = (f32[256,128]{0,1:T(8,128)}, f32[256,128]{0,1:T(8,128)}, u32[]{:S(2)}, u32[]{:S(2)}) collective-permute-start(f32[256,128]{0,1:T(8,128)} %get-tuple-element.18), channel_id=1, source_target_pairs={{0,1},{1,0},{2,3},{3,2},{4,5},{5,4},{6,7},{7,6},{8,9},{9,8},{10,11... | collective-permute-start | bytes 393224 | tf_op jit(solution)/shard_map/ppermute | solution.py:10
  593.7 18.5 %collective-permute-start.21 = (f32[256,128]{0,1:T(8,128)}, f32[256,128]{0,1:T(8,128)}, u32[]{:S(2)}, u32[]{:S(2)}) collective-permute-start(f32[256,128]{0,1:T(8,128)} %get-tuple-element.17), channel_id=1, source_target_pairs={{0,2},{1,3},{2,0},{3,1},{4,6},{5,7},{6,4},{7,5},{8,10},{9,11},{10,... | collective-permute-start | bytes 393224 | tf_op jit(solution)/shard_map/ppermute | solution.py:10
  (33 other events, 2131.0 us)
Sparse Core Ops, SparseCore 0:
  68.3 126.3 all-reduce.3
  414.0 128.8 all-reduce.5
where the time goes:
time: 698 us; the launch traced here: 687 us
  waiting for transfers between devices  256 us (37%)
  blocking collectives  184 us (26%)
  local copies, waits for them, and re-layouts  87.8 us (13%)
  other arithmetic  64.3 us (9%)
  matrix products  48.5 us (7%)
  starting transfers between devices  30.9 us (4%)
  between operations  15.6 us (2%)
    psum x2, waiting for transfers between devices, shards(): summed = lax.psum(spread, ('sub', 'blk'))  254 us
    psum x2, blocking collectives, reduce_rz(): return lax.psum(jnp.sum(left * right, axis=(0, 1)), ('sub', 'blk'))  78.1 us
    all_gather x2, blocking collectives, shards(): whole = lax.all_gather(solved, 'blk', axis=0, tiled=True)  68.2 us
    gather x50, local copies, waits for them, and re-layouts, assemble(): remote = jnp.take(facing, perm_rows[colour], axis=0)  50 us
    unnamed x24, other arithmetic  39.2 us
    psum x1, blocking collectives, shards(): lax.psum(jnp.sum(direction * image, axis=(0, 1)), ('sub', 'blk'))  37.7 us
    dot_general x4, matrix products, local_apply(): jnp.dot(matrix, shaped, precision=lax.Precision.HIGHEST, preferred_elemen...  34.1 us
    ppermute x25, starting transfers between devices, from_partner(): lax.ppermute(array, axis, [(i, i ^ 1 << distance) for i in range(lax.axis...  30.6 us
  transfers between devices with their start and end apart: 27, of which 5 were waited for; matrix products, arithmetic and copies ran while one was open for 9% of the time, Pallas kernels for 0%

commit v1 on v0

v1 whole, which is shorter than its diff:
```python
import functools

import jax
import jax.numpy as jnp
from jax import lax
from jax.experimental import pallas as pl
from jax.experimental.pallas import tpu as pltpu
from jax.sharding import PartitionSpec as P

ITERS = 2
COLOURS = 5
MESH = pl.DeviceIdType.MESH
ORDER = (2, 1, 0, 4, 3)
ARRIVAL = (3, 4, 0, 1, 2)
F32 = jnp.float32
BF16 = jnp.bfloat16


def split(value):
    high = value.astype(BF16)
    low = (value - high.astype(F32)).astype(BF16)
    return high, low


def both(value):
    high, low = split(value)
    return jnp.concatenate([high, low], axis=1)


def mul(left, right):
    return jnp.dot(left, right, preferred_element_type=F32)


def mul3(high, low, pair):
    lanes = pair.shape[1] // 2
    wide = mul(high, pair)
    return wide[:, :lanes] + wide[:, lanes:] + mul(low, pair[:, :lanes])


def fold(value):
    return jnp.sum(value.reshape(value.shape[0] // 8, 8, value.shape[1]), axis=0)


def kernel(
    n_sub, n_blk, group_rows, groups,
    face, mask, dof, dual, dirichlet, coupling, map_rows, map_cols, coarse,
    mult_out, res_out,
    stage, dir_hi, dir_lo, dual_hi, dual_lo, perm,
    coarse_stage, coarse_hi, coarse_lo, m_hi, m_lo, pick,
    cpl_hi, cpl_lo, cplt_hi, cplt_lo,
    vec, res, direc, image, y, step,
    j_send, j_recv, packed, x_recv, y_send, z_recv, d_send, d_recv,
    local_sem, j_ssem, j_rsem, x_ssem, x_rsem, z_ssem, z_rsem, d_ssem, d_rsem,
):
    n = n_sub * n_blk
    my_sub = lax.axis_index("sub")
    my_blk = lax.axis_index("blk")
    me = my_sub * n_blk + my_blk
    dofs = face.shape[2]
    lanes = face.shape[3]
    own = lanes // n_sub
    rows = pick.shape[0]
    width = coarse.shape[1]
    chunk = coarse_stage.shape[0]

    def device(t):
        return (t // n_blk, t % n_blk)

    load_dir = pltpu.make_async_copy(dirichlet.at[0], stage, local_sem.at[0])
    load_dir.start()
    load_coarse = [
        pltpu.make_async_copy(coarse.at[pl.ds(k * chunk, chunk)], coarse_stage, local_sem.at[1])
        for k in range(rows // chunk)
    ]
    load_coarse[0].start()

    barrier = pltpu.get_barrier_semaphore()

    def greet(k, carry):
        pl.semaphore_signal(barrier, inc=1, device_id=device((me + k) % n), device_id_type=MESH)
        return carry

    lax.fori_loop(1, n, greet, 0)

    for c in range(COLOURS):
        places = lax.broadcasted_iota(jnp.int32, (dofs, dofs), 0)
        perm[c] = jnp.where(places == dof[0, c : c + 1, :], 1.0, 0.0).astype(BF16)

    pl.semaphore_wait(barrier, n - 1)

    def partner(c):
        if c < 3:
            hop = 1 << c
            return (my_sub, my_blk + hop - 2 * hop * ((my_blk // hop) % 2))
        hop = 1 << (c - 3)
        return (my_sub + hop - 2 * hop * ((my_sub // hop) % 2), my_blk)

    def j_copy(j, c):
        return pltpu.make_async_remote_copy(
            src_ref=j_send.at[j, c],
            dst_ref=j_recv.at[j, c],
            send_sem=j_ssem.at[j, c],
            recv_sem=j_rsem.at[j, c],
            device_id=partner(c),
            device_id_type=MESH,
        )

    def j_start(j, c, value):
        wide = mul(perm[c], both(value))
        j_send[j, c] = wide[:, :lanes] + wide[:, lanes:]
        j_copy(j, c).start()

    def j_finish(j, c, value):
        j_copy(j, c).wait_recv()
        return mask[0, c].astype(F32) * (value - j_recv[j, c])

    def at(c):
        return pl.ds(c * dofs, dofs)

    def apply(high, low, c):
        return mul3(high[at(c), :], low[at(c), :], vec[...])

    def split_stage(high, low):
        def body(k, carry):
            part = pl.ds(pl.multiple_of(k * 128, 128), 128)
            h, l = split(stage[part, :])
            high[part, :] = h
            low[part, :] = l
            return carry

        lax.fori_loop(0, stage.shape[0] // 128, body, 0)

    def spread(make, count):
        def go(k, carry):
            make((me + k) % n).start()
            return carry

        lax.fori_loop(1, count, go, 0)

    def collect(make, count):
        def go(k, carry):
            make((me + k) % n).wait_recv()
            return carry

        lax.fori_loop(1, count, go, 0)

    def drain(make, count):
        def go(k, carry):
            make((me + k) % n).wait_send()
            return carry

        lax.fori_loop(1, count, go, 0)

    def to(src, dst, ssem, rsem):
        return lambda it, t, pos, landing: pltpu.make_async_remote_copy(
            src_ref=src(it, t), dst_ref=dst.at[it, landing], send_sem=ssem.at[it, t],
            recv_sem=rsem.at[it, pos], device_id=device(t), device_id_type=MESH,
        )

    x_any = to(lambda it, t: packed.at[it, t // n_blk], x_recv, x_ssem, x_rsem)
    z_any = to(lambda it, t: y_send.at[it, t], z_recv, z_ssem, z_rsem)
    d_any = to(lambda it, t: d_send.at[it], d_recv, d_ssem, d_rsem)

    def out(any_copy, it):
        return lambda t: any_copy(it, t, me, me)

    def back(any_copy, it):
        return lambda t: any_copy(it, t, t, t)

    lane = lax.broadcasted_iota(jnp.int32, (group_rows, lanes), 1) // own

    def coarse_send(it, rz_part):
        corner = mul3(cpl_hi[...], cpl_lo[...], vec[...])
        for a in range(n_sub):
            total = jnp.zeros((group_rows, lanes), F32)
            for g in range(groups):
                piece = corner[g * group_rows : (g + 1) * group_rows, :]
                turn = (own * (g - a)) % lanes
                moved = pltpu.roll(piece, turn, 1) if turn else piece
                total = jnp.where(lane == g, moved, total)
            packed[it, a, :group_rows, :] = total
            packed[it, a, group_rows:, :] = rz_part
        spread(out(x_any, it), n)
        x_recv[it, me] = packed[it, my_sub]

    def coarse_solve(it):
        collect(back(x_any, it), n)
        whole = x_recv[it]
        rz = jnp.sum(jnp.sum(whole[:, group_rows:, :], axis=0), axis=0, keepdims=True)
        x = whole[:, :group_rows, :].reshape(n * group_rows, lanes)
        mine = lax.broadcasted_iota(jnp.int32, (n * group_rows, lanes), 1) // own
        total = jnp.zeros((rows, lanes), F32)
        size = n * group_rows
        for g in range(groups):
            wide = mul(pick[:, g * size : (g + 1) * size], both(jnp.where(mine == g, x, 0.0)))
            total = total + wide[:, :lanes] + wide[:, lanes:]
        gathered = total
        for k in range(1, n_sub):
            gathered = gathered + pltpu.roll(total, own * k, 1)
        pair = both(gathered)
        result = jnp.zeros((size, lanes), F32)
        for g in range(groups):
            part = slice(g * size, (g + 1) * size)
            result = jnp.where(mine == g, mul3(m_hi[part, :], m_lo[part, :], pair), result)
        y_send[it] = result.reshape(n, group_rows, lanes)
        spread(out(z_any, it), n)
        z_recv[it, me] = y_send[it, me]
        return rz

    def coarse_back(it):
        collect(back(z_any, it), n)
        sums = [jnp.sum(z_recv[it, a * n_blk : (a + 1) * n_blk], axis=0) for a in range(n_sub)]
        pieces = []
        for g in range(groups):
            total = jnp.zeros((group_rows, lanes), F32)
            for a in range(n_sub):
                turn = (own * (a - g)) % lanes
                moved = pltpu.roll(sums[a], turn, 1) if turn else sums[a]
                total = jnp.where(lane == a, moved, total)
            pieces.append(total)
        return both(jnp.concatenate(pieces, axis=0))

    def dot_send(it, part):
        d_send[it] = part
        spread(out(d_any, it), n)
        d_recv[it, me] = part

    def dot_finish(it):
        collect(back(d_any, it), n)
        return jnp.sum(jnp.sum(d_recv[it], axis=0), axis=0, keepdims=True)

    for c in ORDER:
        j_start(0, c, face[0, c])
    load_dir.wait()
    split_stage(dir_hi, dir_lo)
    load_dual = pltpu.make_async_copy(dual.at[0], stage, local_sem.at[2])
    load_dual.start()
    cpl_hi[...], cpl_lo[...] = split(coupling[0])
    cplt_hi[...], cplt_lo[...] = split(coupling[0].T)
    for c in ARRIVAL:
        r = j_finish(0, c, face[0, c])
        res[c] = r
        vec[at(c), :] = both(r)

    for c in ORDER:
        y[c] = apply(dir_hi, dir_lo, c)
        j_start(1, c, y[c])
    load_dual.wait()
    split_stage(dual_hi, dual_lo)
    for g in range(groups):
        size = n * group_rows
        places = lax.broadcasted_iota(jnp.int32, (rows, size), 0) + my_blk * rows
        pick[:, g * size : (g + 1) * size] = jnp.where(
            places == map_rows[g : g + 1, :], 1.0, 0.0
        ).astype(BF16)
    rz_part = jnp.zeros((8, lanes), F32)
    for c in ARRIVAL:
        p = j_finish(1, c, y[c])
        direc[c] = p
        vec[at(c), :] = both(p)
        rz_part = rz_part + fold(res[c] * p)

    contract_last = (((1,), (1,)), ((), ()))
    alpha = None
    for it in range(ITERS):
        coarse_send(it, rz_part)
        for c in range(COLOURS):
            y[c] = apply(dual_hi, dual_lo, c)
        if it == 0:
            for k in range(rows // chunk):
                if k:
                    load_coarse[k].start()
                load_coarse[k].wait()
                coarse_hi[...], coarse_lo[...] = split(coarse_stage[...])

                def select(i, carry):
                    part = pl.ds(pl.multiple_of(i * 128, 128), 128)
                    places = lax.broadcasted_iota(jnp.int32, (128, width), 1)
                    chosen = jnp.where(places == map_cols[part, 0:1], 1.0, 0.0).astype(BF16)
                    for source, target in ((coarse_hi, m_hi), (coarse_lo, m_lo)):
                        target[part, k * chunk : (k + 1) * chunk] = lax.dot_general(
                            chosen, source[...], contract_last, preferred_element_type=F32
                        ).astype(BF16)
                    return carry

                lax.fori_loop(0, m_hi.shape[0] // 128, select, 0)
        rz_new = coarse_solve(it)
        corners = coarse_back(it)
        for c in ORDER:
            y[c] = y[c] + mul3(cplt_hi[at(c), :], cplt_lo[at(c), :], corners)
            j_start(2 + 2 * it, c, y[c])
        part = jnp.zeros((8, lanes), F32)
        if it == 0:
            rz = rz_new
            for c in ARRIVAL:
                i = j_finish(2, c, y[c])
                image[c] = i
                vec[at(c), :] = both(i)
                part = part + fold(direc[c] * i)
            dot_send(0, part)
            for c in ORDER:
                y[c] = apply(dir_hi, dir_lo, c)
                j_start(3, c, y[c])
            alpha = rz / dot_finish(0)
            rz_part = jnp.zeros((8, lanes), F32)
            for c in ARRIVAL:
                r = res[c] - alpha * image[c]
                res[c] = r
                p = direc[c] - alpha * j_finish(3, c, y[c])
                step[c] = p
                vec[at(c), :] = both(p)
                rz_part = rz_part + fold(r * p)
        else:
            beta = rz_new / rz
            for c in ARRIVAL:
                i = j_finish(4, c, y[c]) + beta * image[c]
                image[c] = i
                p = step[c] + beta * direc[c]
                step[c] = p
                part = part + fold(p * i)
            dot_send(1, part)
            last = rz_new / dot_finish(1)
            for c in range(COLOURS):
                mult_out[0, c] = alpha * direc[c] + last * step[c]
                res_out[0, c] = res[c] - last * image[c]

    for j in range(5):
        for c in range(COLOURS):
            j_copy(j, c).wait_send()
    for it in range(ITERS):
        for any_copy in (x_any, z_any, d_any):
            drain(out(any_copy, it), n)


def solution(mesh):
    n_sub, n_blk = mesh.shape["sub"], mesh.shape["blk"]
    n = n_sub * n_blk

    def shards(face, mask, dof, dual, dirichlet, coupling, corner_map, coarse):
        colours, dofs, lanes = face.shape[1:]
        local = colours * dofs
        corners = corner_map.shape[1]
        group_rows = -(-corners // (8 * n_sub)) * 8
        groups = corners // group_rows
        rows, width = coarse.shape
        chunk = rows if rows <= 192 else 128
        size = n * group_rows
        map_rows = (
            corner_map.reshape(n, groups, group_rows).transpose(1, 0, 2).reshape(groups, size)
        )
        map_cols = jnp.broadcast_to(map_rows.reshape(groups * size, 1), (groups * size, 128))
        vmem = pl.BlockSpec(memory_space=pltpu.VMEM)
        smem = pl.BlockSpec(memory_space=pltpu.SMEM)
        hbm = pl.BlockSpec(memory_space=pl.ANY)
        vector = pltpu.VMEM((colours, dofs, lanes), F32)
        dma = pltpu.SemaphoreType.DMA
        return pl.pallas_call(
            functools.partial(kernel, n_sub, n_blk, group_rows, groups),
            out_shape=[jax.ShapeDtypeStruct(face.shape, F32)] * 2,
            in_specs=[vmem, smem, vmem, hbm, hbm, vmem, vmem, vmem, hbm],
            out_specs=[vmem, vmem],
            scratch_shapes=[
                pltpu.VMEM((local, local), F32),
                pltpu.VMEM((local, local), BF16),
                pltpu.VMEM((local, local), BF16),
                pltpu.VMEM((local, local), BF16),
                pltpu.VMEM((local, local), BF16),
                pltpu.VMEM((colours, dofs, dofs), BF16),
                pltpu.VMEM((chunk, width), F32),
                pltpu.VMEM((chunk, width), BF16),
                pltpu.VMEM((chunk, width), BF16),
                pltpu.VMEM((groups * size, rows), BF16),
                pltpu.VMEM((groups * size, rows), BF16),
                pltpu.VMEM((rows, groups * size), BF16),
                pltpu.VMEM((corners, local), BF16),
                pltpu.VMEM((corners, local), BF16),
                pltpu.VMEM((local, corners), BF16),
                pltpu.VMEM((local, corners), BF16),
                pltpu.VMEM((local, 2 * lanes), BF16),
                vector, vector, vector, vector, vector,
                pltpu.VMEM((5, colours, dofs, lanes), F32),
                pltpu.VMEM((5, colours, dofs, lanes), F32),
                pltpu.VMEM((ITERS, n_sub, group_rows + 8, lanes), F32),
                pltpu.VMEM((ITERS, n, group_rows + 8, lanes), F32),
                pltpu.VMEM((ITERS, n, group_rows, lanes), F32),
                pltpu.VMEM((ITERS, n, group_rows, lanes), F32),
                pltpu.VMEM((ITERS, 8, lanes), F32),
                pltpu.VMEM((ITERS, n, 8, lanes), F32),
                dma((3,)),
                dma((5, colours)), dma((5, colours)),
                dma((ITERS, n)), dma((ITERS, n)),
                dma((ITERS, n)), dma((ITERS, n)),
                dma((ITERS, n)), dma((ITERS, n)),
            ],
            compiler_params=pltpu.CompilerParams(
                collective_id=0, has_side_effects=True, vmem_limit_bytes=62 << 20
            ),
            cost_estimate=pl.CostEstimate(
                flops=3 * 8 * local * local * lanes, bytes_accessed=8 * local * local,
                transcendentals=0,
            ),
        )(face, mask, dof, dual, dirichlet, coupling, map_rows, map_cols, coarse)

    split_first = P(("sub", "blk"), None, None, None)
    return jax.shard_map(
        shards,
        mesh=mesh,
        in_specs=(
            split_first,
            P(("sub", "blk"), None),
            P(("sub", "blk"), None, None),
            P(("sub", "blk"), None, None),
            P(("sub", "blk"), None, None),
            P(("sub", "blk"), None, None),
            P(),
            P("blk", None),
        ),
        out_specs=(split_first, split_first),
        check_vma=False,
    )
```

time: 698 us -> 112 us (0.16); the launches traced: 687 us -> 111 us
  waiting for transfers between devices: 256 us -> 0 us
  blocking collectives: 184 us -> 0 us
  Pallas kernels: 0 us -> 103 us
  local copies, waits for them, and re-layouts: 87.8 us -> 8.03 us
  other arithmetic: 64.3 us -> 0 us
  matrix products: 48.5 us -> 0 us
  starting transfers between devices: 30.9 us -> 0 us
  between operations: 15.6 us -> 0.64 us
    psum x2 -> x0, waiting for transfers between devices: 254 us -> none  [shards(): summed = lax.psum(spread, ('sub', 'blk'))]
    psum x3 -> x0, blocking collectives: 116 us -> none  [the longest x2 78.1 us: reduce_rz(): return lax.psum(jnp.sum(left * right, axis=(0, 1)), ('sub', 'blk'))]
    pallas_call x0 -> x1, Pallas kernels: none -> 103 us  [shards(): pl.pallas_call(functools.partial(kernel, n_sub, n_blk, group_rows, groups...]
    all_gather x2 -> x0, blocking collectives: 68.2 us -> none  [shards(): whole = lax.all_gather(solved, 'blk', axis=0, tiled=True)]
    gather x52 -> x0, local copies, waits for them, and re-layouts: 53.6 us -> none  [the longest x50 50 us: assemble(): remote = jnp.take(facing, perm_rows[colour], axis=0)]
    dot_general x12 -> x0, matrix products: 48.5 us -> none  [the longest x4 34.1 us: local_apply(): jnp.dot(matrix, shaped, precision=lax.Precision.HIGHEST, preferred_elemen...]
    unnamed x24 -> x0, other arithmetic: 39.2 us -> none
    ppermute x25 -> x0, starting transfers between devices: 30.6 us -> none  [from_partner(): lax.ppermute(array, axis, [(i, i ^ 1 << distance) for i in range(lax.axis...]
  transfers between devices with their start and end apart: 27 -> 0, of which waited for: 5 -> 0; matrix products, arithmetic and copies ran while one was open for 9% -> 0% of each run, Pallas kernels for 0% -> 0%
where the time goes in v1:
time: 112 us; the launch traced here: 111 us
  Pallas kernels  103 us (92%)
  local copies, waits for them, and re-layouts  8.03 us (7%)
    pallas_call x1, Pallas kernels, shards(): pl.pallas_call(functools.partial(kernel, n_sub, n_blk, group_rows, groups...  103 us
    unnamed x4, local copies, waits for them, and re-layouts  6.01 us

profile of v1, /device:TPU:0, one launch (start us, length us, event | category | flops | bytes accessed | tf_op | source)
XLA Modules:
  0.0 111.5 jit_solution(1460048628658706593)
XLA Ops:
  0.6 1.3 %copy.15.dof = s32[1,5,256]{2,1,0:T(8,128)} copy(s32[1,5,256]{2,0,1:T(1,128)} %param.10) | data formatting | bytes 10240 | tf_op args[2]
  1.9 0.8 copy.12
  2.7 0.1 copy.13
  2.8 0.1 broadcast_in_dim.7
  2.9 0.7 reshape.12.map_rows
  3.6 1.2 %broadcast_in_dim.8.map_cols = s32[1536,128]{1,0:T(8,128)} broadcast(s32[1536]{0:T(1024)S(1)} %broadcast_in_dim.7), dimensions={0} | broadcast | bytes 792576 | tf_op jit(solution)/shard_map/broadcast_in_dim | solution.py:351
  4.7 102.8 %shard_map.95 = (f32[1,5,256,128]{3,2,1,0:T(8,128)}, f32[1,5,256,128]{3,2,1,0:T(8,128)}) custom-call(f32[1,5,256,128]{3,2,1,0:T(8,128)} %face.1, s32[1,5]{1,0:T(1,128)} %mask.1, s32[1,5,256]{2,1,0:T(8,128)} %copy.15.dof, f32[1,1280,1280]{2,1,0:T(8,128)} %dual.1, f32[1,1280,1280]{2,1,0:T(8,128)} %dirichlet.1, f32[1,48,1280]{2,1,0:T(8,128)} %coupling.1, ...), custom_call_target="tpu_custom_call" | custom-call | flops 5033164800 | bytes 13107200 | tf_op jit(solution)/shard_map/pallas_call | solution.py:357
  107.5 2.0 %copy.18 = f32[1,5,256,128]{3,2,1,0:T(8,128)} copy(f32[1,5,256,128]{3,2,1,0:T(8,128)} %get-tuple-element.4) | data formatting | bytes 1310720
  109.5 2.0 %copy.19 = f32[1,5,256,128]{3,2,1,0:T(8,128)} copy(f32[1,5,256,128]{3,2,1,0:T(8,128)} %get-tuple-element.5) | data formatting | bytes 1310720

commit v2 on v1

--- a/solution.py
+++ b/solution.py
@@ -44,11 +44,11 @@
 def kernel(
     n_sub, n_blk, group_rows, groups,
     face, mask, dof, dual, dirichlet, coupling, map_rows, map_cols, coarse,
-    mult_out, res_out,
+    direc, step, res, image, scales,
     stage, dir_hi, dir_lo, dual_hi, dual_lo, perm,
     coarse_stage, coarse_hi, coarse_lo, m_hi, m_lo, pick,
     cpl_hi, cpl_lo, cplt_hi, cplt_lo,
-    vec, res, direc, image, y, step,
+    vec, y, y_next,
     j_send, j_recv, packed, x_recv, y_send, z_recv, d_send, d_recv,
     local_sem, j_ssem, j_rsem, x_ssem, x_rsem, z_ssem, z_rsem, d_ssem, d_rsem,
 ):
@@ -63,8 +63,16 @@
     width = coarse.shape[1]
     chunk = coarse_stage.shape[0]
 
-    def device(t):
-        return (t // n_blk, t % n_blk)
+    def visit(act):
+        for k in range(n_sub):
+            sub_to = lax.rem(my_sub + k, n_sub)
+
+            def go(j, carry):
+                blk_to = lax.rem(my_blk + j, n_blk)
+                act(sub_to, blk_to, sub_to * n_blk + blk_to)
+                return carry
+
+            lax.fori_loop(0 if k else 1, n_blk, go, 0)
 
     load_dir = pltpu.make_async_copy(dirichlet.at[0], stage, local_sem.at[0])
     load_dir.start()
@@ -76,15 +84,15 @@
 
     barrier = pltpu.get_barrier_semaphore()
 
-    def greet(k, carry):
-        pl.semaphore_signal(barrier, inc=1, device_id=device((me + k) % n), device_id_type=MESH)
-        return carry
-
-    lax.fori_loop(1, n, greet, 0)
+    visit(
+        lambda a, b, t: pl.semaphore_signal(
+            barrier, inc=1, device_id=(a, b), device_id_type=MESH
+        )
+    )
 
     for c in range(COLOURS):
         places = lax.broadcasted_iota(jnp.int32, (dofs, dofs), 0)
-        perm[c] = jnp.where(places == dof[0, c : c + 1, :], 1.0, 0.0).astype(BF16)
+        perm[c] = jnp.where(places == dof[c], 1.0, 0.0).astype(BF16)
 
     pl.semaphore_wait(barrier, n - 1)
 
@@ -130,64 +138,59 @@
 
         lax.fori_loop(0, stage.shape[0] // 128, body, 0)
 
-    def spread(make, count):
-        def go(k, carry):
-            make((me + k) % n).start()
-            return carry
-
-        lax.fori_loop(1, count, go, 0)
-
-    def collect(make, count):
-        def go(k, carry):
-            make((me + k) % n).wait_recv()
-            return carry
-
-        lax.fori_loop(1, count, go, 0)
-
-    def drain(make, count):
-        def go(k, carry):
-            make((me + k) % n).wait_send()
-            return carry
-
-        lax.fori_loop(1, count, go, 0)
-
-    def to(src, dst, ssem, rsem):
-        return lambda it, t, pos, landing: pltpu.make_async_remote_copy(
-            src_ref=src(it, t), dst_ref=dst.at[it, landing], send_sem=ssem.at[it, t],
-            recv_sem=rsem.at[it, pos], device_id=device(t), device_id_type=MESH,
+    def exchange(source, target, ssem, rsem):
+        def copy(it, a, b, t, landing):
+            return pltpu.make_async_remote_copy(
+                src_ref=source(it, a, t), dst_ref=target.at[it, landing],
+                send_sem=ssem.at[it, t], recv_sem=rsem.at[it, landing],
+                device_id=(a, b), device_id_type=MESH,
+            )
+
+        return (
+            lambda it: visit(lambda a, b, t: copy(it, a, b, t, me).start()),
+            lambda it: visit(lambda a, b, t: copy(it, a, b, t, t).wait_recv()),
+            lambda it: visit(lambda a, b, t: copy(it, a, b, t, me).wait_send()),
         )
 
-    x_any = to(lambda it, t: packed.at[it, t // n_blk], x_recv, x_ssem, x_rsem)
-    z_any = to(lambda it, t: y_send.at[it, t], z_recv, z_ssem, z_rsem)
-    d_any = to(lambda it, t: d_send.at[it], d_recv, d_ssem, d_rsem)
-
-    def out(any_copy, it):
-        return lambda t: any_copy(it, t, me, me)
-
-    def back(any_copy, it):
-        return lambda t: any_copy(it, t, t, t)
+    x_start, x_wait, x_drain = exchange(
+        lambda it, a, t: packed.at[it, a], x_recv, x_ssem, x_rsem
+    )
+    z_start, z_wait, z_drain = exchange(lambda it, a, t: y_send.at[it, t], z_recv, z_ssem, z_rsem)
+    d_start, d_wait, d_drain = exchange(lambda it, a, t: d_send.at[it], d_recv, d_ssem, d_rsem)
 
     lane = lax.broadcasted_iota(jnp.int32, (group_rows, lanes), 1) // own
 
     def coarse_send(it, rz_part):
         corner = mul3(cpl_hi[...], cpl_lo[...], vec[...])
+        rz_sum = jnp.sum(rz_part, axis=0, keepdims=True)
+        row = lax.broadcasted_iota(jnp.int32, (group_rows, lanes), 0)
+        rz_rows = jnp.zeros((group_rows, lanes), F32)
+        for k in range(n_sub):
+            turn = (own * (groups - k)) % lanes
+            moved = pltpu.roll(jnp.broadcast_to(rz_sum, (8, lanes)), turn, 1)[0:1, :]
+            rz_rows = jnp.where((row == k) & (lane == groups), moved, rz_rows)
         for a in range(n_sub):
-            total = jnp.zeros((group_rows, lanes), F32)
+            total = rz_rows
             for g in range(groups):
                 piece = corner[g * group_rows : (g + 1) * group_rows, :]
                 turn = (own * (g - a)) % lanes
                 moved = pltpu.roll(piece, turn, 1) if turn else piece
                 total = jnp.where(lane == g, moved, total)
-            packed[it, a, :group_rows, :] = total
-            packed[it, a, group_rows:, :] = rz_part
-        spread(out(x_any, it), n)
+            packed[it, a] = total
+        x_start(it)
         x_recv[it, me] = packed[it, my_sub]
 
     def coarse_solve(it):
-        collect(back(x_any, it), n)
+        x_wait(it)
         whole = x_recv[it]
-        rz = jnp.sum(jnp.sum(whole[:, group_rows:, :], axis=0), axis=0, keepdims=True)
-        x = whole[:, :group_rows, :].reshape(n * group_rows, lanes)
+        rz_rows = jnp.sum(whole, axis=0)
+        rz = jnp.zeros((group_rows, lanes), F32)
+        for k in range(n_sub):
+            turn = (own * (k - groups)) % lanes
+            moved = pltpu.roll(rz_rows, turn, 1)
+            rz = jnp.where(lane == k, moved[k : k + 1, :], rz)
+        rz = rz[0:1, :]
+        x = whole.reshape(n * group_rows, lanes)
         mine = lax.broadcasted_iota(jnp.int32, (n * group_rows, lanes), 1) // own
         total = jnp.zeros((rows, lanes), F32)
         size = n * group_rows
@@ -203,12 +206,12 @@
             part = slice(g * size, (g + 1) * size)
             result = jnp.where(mine == g, mul3(m_hi[part, :], m_lo[part, :], pair), result)
         y_send[it] = result.reshape(n, group_rows, lanes)
-        spread(out(z_any, it), n)
+        z_start(it)
         z_recv[it, me] = y_send[it, me]
         return rz
 
     def coarse_back(it):
-        collect(back(z_any, it), n)
+        z_wait(it)
         sums = [jnp.sum(z_recv[it, a * n_blk : (a + 1) * n_blk], axis=0) for a in range(n_sub)]
         pieces = []
         for g in range(groups):
@@ -221,13 +224,21 @@
         return both(jnp.concatenate(pieces, axis=0))
 
     def dot_send(it, part):
-        d_send[it] = part
-        spread(out(d_any, it), n)
-        d_recv[it, me] = part
+        total = jnp.sum(part, axis=0, keepdims=True)
+        d_send[it] = total
+        d_start(it)
+        d_recv[it, me] = total
 
     def dot_finish(it):
-        collect(back(d_any, it), n)
-        return jnp.sum(jnp.sum(d_recv[it], axis=0), axis=0, keepdims=True)
+        d_wait(it)
+        return jnp.sum(d_recv[it], axis=0)
+
+    def absorb(high, low, index, c, value, target):
+        pair = both(value)
+        for k in ORDER:
+            part = mul3(high[at(k), at(c)], low[at(k), at(c)], pair)
+            target[k] = part if index == 0 else target[k] + part
+            yield k
 
     for c in ORDER:
         j_start(0, c, face[0, c])
@@ -237,22 +248,33 @@
     load_dual.start()
     cpl_hi[...], cpl_lo[...] = split(coupling[0])
     cplt_hi[...], cplt_lo[...] = split(coupling[0].T)
-    for c in ARRIVAL:
+    for index, c in enumerate(ARRIVAL):
         r = j_finish(0, c, face[0, c])
         res[c] = r
-        vec[at(c), :] = both(r)
-
-    for c in ORDER:
-        y[c] = apply(dir_hi, dir_lo, c)
-        j_start(1, c, y[c])
+        for k in absorb(dir_hi, dir_lo, index, c, r, y):
+            if index == COLOURS - 1:
+                j_start(1, k, y[k])
     load_dual.wait()
     split_stage(dual_hi, dual_lo)
-    for g in range(groups):
-        size = n * group_rows
-        places = lax.broadcasted_iota(jnp.int32, (rows, size), 0) + my_blk * rows
-        pick[:, g * size : (g + 1) * size] = jnp.where(
-            places == map_rows[g : g + 1, :], 1.0, 0.0
-        ).astype(BF16)
+    contract_last = (((1,), (1,)), ((), ()))
+    for k in range(rows // chunk):
+        if k:
+            load_coarse[k].start()
+        load_coarse[k].wait()
+        coarse_hi[...], coarse_lo[...] = split(coarse_stage[...])
+        batch = 512 if width <= 2048 else 128
+
+        def select(i, carry):
+            part = pl.ds(pl.multiple_of(i * batch, batch), batch)
+            places = lax.broadcasted_iota(jnp.int32, (batch, width), 1)
+            chosen = jnp.where(places == map_cols[part, 0:1], 1.0, 0.0).astype(BF16)
+            for source, target in ((coarse_hi, m_hi), (coarse_lo, m_lo)):
+                target[part, k * chunk : (k + 1) * chunk] = lax.dot_general(
+                    chosen, source[...], contract_last, preferred_element_type=F32
+                ).astype(BF16)
+            return carry
+
+        lax.fori_loop(0, m_hi.shape[0] // batch, select, 0)
     rz_part = jnp.zeros((8, lanes), F32)
     for c in ARRIVAL:
         p = j_finish(1, c, y[c])
@@ -260,30 +282,18 @@
         vec[at(c), :] = both(p)
         rz_part = rz_part + fold(res[c] * p)
 
-    contract_last = (((1,), (1,)), ((), ()))
     alpha = None
     for it in range(ITERS):
         coarse_send(it, rz_part)
         for c in range(COLOURS):
             y[c] = apply(dual_hi, dual_lo, c)
         if it == 0:
-            for k in range(rows // chunk):
-                if k:
-                    load_coarse[k].start()
-                load_coarse[k].wait()
-                coarse_hi[...], coarse_lo[...] = split(coarse_stage[...])
-
-                def select(i, carry):
-                    part = pl.ds(pl.multiple_of(i * 128, 128), 128)
-                    places = lax.broadcasted_iota(jnp.int32, (128, width), 1)
-                    chosen = jnp.where(places == map_cols[part, 0:1], 1.0, 0.0).astype(BF16)
-                    for source, target in ((coarse_hi, m_hi), (coarse_lo, m_lo)):
-                        target[part, k * chunk : (k + 1) * chunk] = lax.dot_general(
-                            chosen, source[...], contract_last, preferred_element_type=F32
-                        ).astype(BF16)
-                    return carry
-
-                lax.fori_loop(0, m_hi.shape[0] // 128, select, 0)
+            for g in range(groups):
+                size = n * group_rows
+                places = lax.broadcasted_iota(jnp.int32, (rows, size), 0) + my_blk * rows
+                pick[:, g * size : (g + 1) * size] = jnp.where(
+                    places == map_rows[g : g + 1, :], 1.0, 0.0
+                ).astype(BF16)
         rz_new = coarse_solve(it)
         corners = coarse_back(it)
         for c in ORDER:
@@ -292,21 +302,20 @@
         part = jnp.zeros((8, lanes), F32)
         if it == 0:
             rz = rz_new
-            for c in ARRIVAL:
+            for index, c in enumerate(ARRIVAL):
                 i = j_finish(2, c, y[c])
                 image[c] = i
-                vec[at(c), :] = both(i)
                 part = part + fold(direc[c] * i)
+                for k in absorb(dir_hi, dir_lo, index, c, i, y_next):
+                    if index == COLOURS - 1:
+                        j_start(3, k, y_next[k])
             dot_send(0, part)
-            for c in ORDER:
-                y[c] = apply(dir_hi, dir_lo, c)
-                j_start(3, c, y[c])
             alpha = rz / dot_finish(0)
             rz_part = jnp.zeros((8, lanes), F32)
             for c in ARRIVAL:
                 r = res[c] - alpha * image[c]
                 res[c] = r
-                p = direc[c] - alpha * j_finish(3, c, y[c])
+                p = direc[c] - alpha * j_finish(3, c, y_next[c])
                 step[c] = p
                 vec[at(c), :] = both(p)
                 rz_part = rz_part + fold(r * p)
@@ -320,16 +329,16 @@
                 part = part + fold(p * i)
             dot_send(1, part)
             last = rz_new / dot_finish(1)
-            for c in range(COLOURS):
-                mult_out[0, c] = alpha * direc[c] + last * step[c]
-                res_out[0, c] = res[c] - last * image[c]
+            scales[0:1, :] = alpha
+            scales[1:2, :] = last
 
     for j in range(5):
         for c in range(COLOURS):
             j_copy(j, c).wait_send()
     for it in range(ITERS):
-        for any_copy in (x_any, z_any, d_any):
-            drain(out(any_copy, it), n)
+        x_drain(it)
+        z_drain(it)
+        d_drain(it)
 
 
 def solution(mesh):
@@ -354,11 +363,12 @@
         hbm = pl.BlockSpec(memory_space=pl.ANY)
         vector = pltpu.VMEM((colours, dofs, lanes), F32)
         dma = pltpu.SemaphoreType.DMA
-        return pl.pallas_call(
+        direc, step, res, image, scales = pl.pallas_call(
             functools.partial(kernel, n_sub, n_blk, group_rows, groups),
-            out_shape=[jax.ShapeDtypeStruct(face.shape, F32)] * 2,
+            out_shape=[jax.ShapeDtypeStruct(face.shape[1:], F32)] * 4
+            + [jax.ShapeDtypeStruct((2, lanes), F32)],
             in_specs=[vmem, smem, vmem, hbm, hbm, vmem, vmem, vmem, hbm],
-            out_specs=[vmem, vmem],
+            out_specs=[vmem] * 5,
             scratch_shapes=[
                 pltpu.VMEM((local, local), F32),
                 pltpu.VMEM((local, local), BF16),
@@ -377,15 +387,15 @@
                 pltpu.VMEM((local, corners), BF16),
                 pltpu.VMEM((local, corners), BF16),
                 pltpu.VMEM((local, 2 * lanes), BF16),
-                vector, vector, vector, vector, vector,
+                vector, vector,
                 pltpu.VMEM((5, colours, dofs, lanes), F32),
                 pltpu.VMEM((5, colours, dofs, lanes), F32),
-                pltpu.VMEM((ITERS, n_sub, group_rows + 8, lanes), F32),
-                pltpu.VMEM((ITERS, n, group_rows + 8, lanes), F32),
+                pltpu.VMEM((ITERS, n_sub, group_rows, lanes), F32),
                 pltpu.VMEM((ITERS, n, group_rows, lanes), F32),
                 pltpu.VMEM((ITERS, n, group_rows, lanes), F32),
-                pltpu.VMEM((ITERS, 8, lanes), F32),
-                pltpu.VMEM((ITERS, n, 8, lanes), F32),
+                pltpu.VMEM((ITERS, n, group_rows, lanes), F32),
+                pltpu.VMEM((ITERS, 1, lanes), F32),
+                pltpu.VMEM((ITERS, n, 1, lanes), F32),
                 dma((3,)),
                 dma((5, colours)), dma((5, colours)),
                 dma((ITERS, n)), dma((ITERS, n)),
@@ -399,7 +409,9 @@
                 flops=3 * 8 * local * local * lanes, bytes_accessed=8 * local * local,
                 transcendentals=0,
             ),
-        )(face, mask, dof, dual, dirichlet, coupling, map_rows, map_cols, coarse)
+        )(face, mask, dof.transpose(1, 0, 2), dual, dirichlet, coupling, map_rows, map_cols, coarse)
+        alpha, last = scales[0], scales[1]
+        return (alpha * direc + last * step)[None], (res - last * image)[None]
 
     split_first = P(("sub", "blk"), None, None, None)
     return jax.shard_map(

time: 112 us -> 105 us (0.938)
  Pallas kernels: 103 us -> 98.1 us
  local copies, waits for them, and re-layouts: 8.03 us -> 3.57 us
  other arithmetic: 0 us -> 2.87 us
    unnamed x4 -> x1, local copies, waits for them, and re-layouts: 6.01 us -> 0.79 us
    pallas_call x1, Pallas kernels: 103 us -> 98.1 us  [shards(): pl.pallas_call(functools.partial(kernel, n_sub, n_blk, group_rows, groups...]
    broadcast_in_dim x0 -> x1, other arithmetic: none -> 2.87 us  [shards(): return ((alpha * direc + last * step)[None], (res - last * image)[None])]
where the time goes in v2:
time: 105 us
  Pallas kernels  98.1 us (93%)
  local copies, waits for them, and re-layouts  3.57 us (3%)
  other arithmetic  2.87 us (3%)
    pallas_call x1, Pallas kernels, shards(): pl.pallas_call(functools.partial(kernel, n_sub, n_blk, group_rows, groups...  98.1 us
    broadcast_in_dim x1, other arithmetic, shards(): return ((alpha * direc + last * step)[None], (res - last * image)[None])  2.87 us

profile of v2, /device:TPU:0, one launch (start us, length us, event | category | flops | bytes accessed | tf_op | source)
XLA Modules:
  0.0 105.2 jit_solution(1050424947509622361)
XLA Ops:
  0.6 0.8 copy.11
  1.4 0.1 copy.12
  1.5 0.1 broadcast_in_dim.13
  1.6 0.7 reshape.14.map_rows
  2.3 1.2 %broadcast_in_dim.14.map_cols = s32[1536,128]{1,0:T(8,128)} broadcast(s32[1536]{0:T(1024)S(1)} %broadcast_in_dim.13), dimensions={0} | broadcast | bytes 792576 | tf_op jit(solution)/shard_map/broadcast_in_dim | solution.py:360
  3.4 98.1 %shard_map.95 = (f32[5,256,128]{2,1,0:T(8,128)}, f32[5,256,128]{2,1,0:T(8,128)}, f32[5,256,128]{2,1,0:T(8,128)}, f32[5,256,128]{2,1,0:T(8,128)}, f32[2,128]{1,0:T(2,128)}) custom-call(f32[1,5,256,128]{3,2,1,0:T(8,128)} %face.1, s32[1,5]{1,0:T(1,128)} %mask.1, s32[5,1,256]{2,1,0:T(1,128)} %bitcast.13, f32[1,1280,1280]{2,1,0:T(8,128)} %dual.1, ...), custom_call_target="tpu_custom_call" | custom-call | flops 5033164800 | bytes 13107200 | tf_op jit(solution)/shard_map/pallas_call | solution.py:366
  101.6 0.7 slice_bitcast_fusion.1
  102.3 2.9 %subtract_bitcast_fusion = (f32[1,5,256,128]{3,2,1,0:T(8,128)}, f32[1,5,256,128]{3,2,1,0:T(8,128)}) fusion(f32[5,256,128]{2,1,0:T(8,128)} %get-tuple-element.10, f32[5,256,128]{2,1,0:T(8,128)} %get-tuple-element.11, f32[128]{0:T(128)S(1)} %get-tuple-element.13, f32[5,256,128]{2,1,0:T(8,128)} %get-tuple-element.9, f32[5,256,128]{2,1,0:T(8,128)} %get-tuple-element.8, ...), kind=kLoop, calls=%fused_computation | loop fusion | flops 819200 | bytes 3933184 | tf_op jit(solution)/shard_map/broadcast_in_dim | solution.py:414
